TPU v7x, 32 devices: a whole 2x2x4 slice. The times are simulated.
32 devices in a mesh: pipe: 4 (over x, core), dp: 2 (over y), vocab: 4 (over z).
Axes of the slice: x: 2, y: 2, z: 4, core: 2. Of those that a mesh axis runs over, the one named last changes fastest.
Arguments:
- hidden: bfloat16 [512, 4608], P(('pipe', 'dp', 'vocab')), may hold values from -6 to 6
- targets: int32 [512], P(('pipe', 'dp', 'vocab')), may hold values from 0 to 12287, as said below
- input_ids: int32 [512], P(('pipe', 'dp', 'vocab')), may hold values from 0 to 12287, as said below
- input_grads: bfloat16 [512, 4608], P(('pipe', 'dp', 'vocab')), may hold values from -0.3125 to 0.3125
- table: bfloat16 [12288, 4608], P(('pipe', 'vocab'), 'dp'), may hold values from -0.75 to 0.75
- keep: int32 [12288], P(('pipe', 'vocab')), may hold values from 0 to 1
- first_moment: bfloat16 [12288, 4608], P(('pipe', 'vocab'), 'dp'), may hold values from -0.015625 to 0.015625
- second_moment: bfloat16 [12288, 4608], P(('pipe', 'vocab'), 'dp'), may hold values from 9.983778e-07 to 9.953976e-06
Outputs:
- new_table: bfloat16 [12288, 4608], P(('pipe', 'vocab'), 'dp')
- new_first: bfloat16 [12288, 4608], P(('pipe', 'vocab'), 'dp')
- new_second: bfloat16 [12288, 4608], P(('pipe', 'vocab'), 'dp')
- loss: float32 [], replicated
Inputs may be any that keep to these rules, and one draw needn't show every extreme that they name: `targets`: names only rows with keep = 1. `input_ids`: names only rows with keep = 1.
All inputs are finite; a program needn't handle non-finite values.
Results may differ from a plain program's by a relative error of at most 0.0036.
Values may be sent and summed in bfloat16 or wider, within the bound.
A program may use at most 192 MiB of HBM per device.

v0:
```python
import math
import jax
import jax.numpy as jnp
from jax import lax
from jax.sharding import PartitionSpec as P

SOFTCAP = 30.0
LEARN = 0.01
EPSILON = 1e-08


def contract_last(left, right):
    return lax.dot_general(
        left, right, (((1,), (1,)), ((), ())), preferred_element_type=jnp.float32
    )


def contract_first(left, right):
    return lax.dot_general(
        left, right, (((0,), (0,)), ((), ())), preferred_element_type=jnp.float32
    )


def body(hidden, targets, input_ids, input_grads, table, keep, first_moment, second_moment):
    rows_here = table.shape[0]
    row_start = lax.axis_index(("pipe", "vocab")) * rows_here
    keepf = keep.astype(jnp.float32)
    scale = math.sqrt(hidden.shape[1])
    groups_dp = lax.axis_size("dp")
    row_iota = jnp.arange(rows_here, dtype=jnp.int32)
    both = jnp.stack([targets, input_ids])
    packed = lax.all_to_all(
        jnp.stack([hidden, input_grads]), "dp", split_axis=2, concat_axis=1, tiled=True
    )
    ids_all = lax.all_gather(both, ("pipe", "vocab", "dp"), axis=1, tiled=True)
    tokens_all = lax.all_gather(packed[0], ("pipe", "vocab"), axis=0, tiled=True)
    grads_all = lax.all_gather(packed[1], ("pipe", "vocab"), axis=0, tiled=True)
    tokens = tokens_all.shape[0]
    share = tokens // groups_dp
    start = lax.axis_index("dp") * share
    goals = lax.dynamic_slice(ids_all[0], (start,), (share,))
    raw = lax.psum_scatter(contract_last(tokens_all, table), "dp", scatter_dimension=0, tiled=True)
    capped = SOFTCAP * jnp.tanh(raw / SOFTCAP)
    onehot = ((goals - row_start)[:, None] == row_iota[None, :]).astype(jnp.float32)
    weights = jnp.exp(capped) * keepf[None, :]
    local = jnp.stack([jnp.sum(weights, axis=1), jnp.sum(capped * onehot, axis=1)])
    placed = lax.dynamic_update_slice(jnp.zeros((2, tokens), jnp.float32), local, (0, start))
    sums = lax.psum(placed, ("pipe", "dp", "vocab"))
    token_loss = jnp.sum(jnp.log(sums[0]) - sums[1])
    total = lax.dynamic_slice(sums[0], (start,), (share,))
    slope = 1.0 - (capped / SOFTCAP) ** 2
    dlogits = ((weights / total[:, None] - onehot) * slope).astype(jnp.bfloat16)
    dlogits = lax.all_gather(dlogits, "dp", axis=0, tiled=True)
    selector = ((ids_all[1] - row_start)[None, :] == row_iota[:, None]).astype(jnp.bfloat16)
    finished = contract_first(dlogits, tokens_all) + scale * jnp.dot(
        selector, grads_all, preferred_element_type=jnp.float32
    )
    kept = keep[:, None] > 0
    first_new = (0.9 * first_moment.astype(jnp.float32) + 0.1 * finished).astype(jnp.bfloat16)
    second_new = (0.95 * second_moment.astype(jnp.float32) + 0.05 * finished * finished).astype(
        jnp.bfloat16
    )
    corr_one = 1.0 - 0.9**10
    corr_two = 1.0 - 0.95**10
    update = (
        first_new.astype(jnp.float32)
        / corr_one
        / (jnp.sqrt(second_new.astype(jnp.float32) / corr_two) + EPSILON)
    )
    table_new = (table.astype(jnp.float32) - LEARN * update).astype(jnp.bfloat16)
    new_table = jnp.where(kept, table_new, table)
    new_first = jnp.where(kept, first_new, first_moment)
    new_second = jnp.where(kept, second_new, second_moment)
    return (new_table, new_first, new_second, token_loss)


def solution(mesh):
    placed = (
        P(("pipe", "dp", "vocab"), None),
        P(("pipe", "dp", "vocab")),
        P(("pipe", "dp", "vocab")),
        P(("pipe", "dp", "vocab"), None),
        P(("pipe", "vocab"), "dp"),
        P(("pipe", "vocab")),
        P(("pipe", "vocab"), "dp"),
        P(("pipe", "vocab"), "dp"),
    )
    return jax.shard_map(
        body,
        mesh=mesh,
        in_specs=placed,
        out_specs=(
            P(("pipe", "vocab"), "dp"),
            P(("pipe", "vocab"), "dp"),
            P(("pipe", "vocab"), "dp"),
            P(),
        ),
        check_vma=False,
    )
```

profile of v0, /device:TPU:10, one launch (start us, length us, event | category | flops | bytes accessed | tf_op | source)
XLA Modules:
  0.0 227.2 jit_solution(489731304706484116)
XLA Ops:
  7.2 0.0 all-gather.4.cloned.1.call-start
  7.2 1.0 pad_maximum_fusion
  8.2 3.0 %copy.27 = bf16[2,16,4608]{1,0,2:T(2,128)(2,1)S(1)} copy(bf16[2,16,4608]{2,1,0:T(8,128)(2,1)S(1)} %pad_maximum_fusion) | data formatting | bytes 589824 | tf_op jit(solution)/shard_map/stack | solution.py:33
  11.2 2.5 %reshape.30 = bf16[2,2,36864]{2,1,0:T(2,128)(2,1)S(1)} reshape(bf16[4608,2,16]{2,1,0:T(2,128)(2,1)S(1)} %bitcast.27) | data formatting | bytes 589824
  13.7 8.2 %all_to_all.15 = bf16[2,2,36864]{2,1,0:T(2,128)(2,1)S(1)} all-to-all(bf16[2,2,36864]{2,1,0:T(2,128)(2,1)S(1)} %reshape.30), channel_id=1, replica_groups=mesh['pipe'=4,'dp'=2,'vocab'=4] {'dp'}, dimensions={0} | all-to-all | bytes 589824 | tf_op jit(solution)/shard_map/all_to_all | solution.py:32
  21.9 1.6 reshape.31
  23.5 1.6 copy.32
  25.1 0.2 fusion.6
  25.3 0.7 copy.29
  26.0 0.0 all-gather.4.cloned.1.call-update
  26.0 0.0 copy-start.1
  26.0 0.0 copy-start.2
  26.0 0.0 copy-start.3
  26.1 0.0 reduce-scatter.2.cloned.1.call-start
  26.1 41.0 %all-gather.4.cloned.1.call-done = bf16[512,2304]{1,0:T(8,128)(2,1)} async-done(((bf16[32,2304]{1,0:T(8,128)(2,1)}), bf16[512,2304]{1,0:T(8,128)(2,1)}) %all-gather.4.cloned.1.call-update) | async-done | bytes 2359312 | tf_op jit(solution)/shard_map/all_gather | solution.py:36
  67.2 5.9 %fusion.7 = f32[512,768]{1,0:T(8,128)} fusion(bf16[512,2304]{1,0:T(8,128)(2,1)} %all-gather.4.cloned.1.call-done, bf16[768,2304]{1,0:T(8,128)(2,1)} %param.12), kind=kOutput, calls=%fused_computation.27 | convolution fusion | flops 1811939328 | bytes 7471104 | tf_op jit(solution)/shard_map/dot_general | solution.py:13
  73.0 0.0 copy-start
  73.0 0.0 reduce-scatter.2.cloned.1.call-update
  73.1 0.0 all-gather.6.cloned.1.call-start
  73.1 0.7 copy.31
  73.8 0.0 all-gather.6.cloned.1.call-update
  73.8 0.0 copy-done.1
  73.8 0.0 copy-done.2
  73.9 0.0 copy-done.3
  73.9 65.0 %all-gather = s32[32,16,2]{1,2,0:T(2,128)S(1)} all-gather(s32[1,16,2]{1,2,0:T(2,128)S(1)} %add_bitcast_fusion), channel_id=1, replica_groups=mesh['pipe'=4,'dp'=2,'vocab'=4] {'pipe','vocab','dp'}, dimensions={0}, use_global_device_ids=true | all-gather | bytes 4224 | tf_op jit(solution)/shard_map/all_gather | solution.py:35
  138.8 0.1 reshape.29
  139.0 0.0 reduce-scatter.2.cloned.1.call-done
  139.0 1.6 fusion.4
  140.7 42.0 %psum.7 = f32[2,512]{1,0:T(2,128)S(1)} all-reduce(f32[2,512]{1,0:T(2,128)S(1)} %maximum_dynamic-update-slice_fusion), channel_id=1, replica_groups=mesh['pipe'=4,'dp'=2,'vocab'=4] {'pipe','dp','vocab'}, use_global_device_ids=true, to_apply=%region_3.0 | all-reduce | flops 1024 | bytes 8192 | tf_op jit(solution)/shard_map/psum | solution.py:48
  182.6 0.6 fusion.5
  183.2 1.5 multiply_convert_fusion
  184.8 10.6 %all_gather.14 = bf16[512,768]{1,0:T(8,128)(2,1)S(1)} all-gather(bf16[256,768]{1,0:T(8,128)(2,1)S(1)} %multiply_convert_fusion), channel_id=1, replica_groups=mesh['pipe'=4,'dp'=2,'vocab'=4] {'dp'}, dimensions={0}, use_global_device_ids=true | all-gather | bytes 1179648 | tf_op jit(solution)/shard_map/all_gather | solution.py:53
  195.4 0.0 copy-done
  195.4 5.0 %fusion.8 = f32[768,2304]{1,0:T(8,128)} fusion(bf16[512,768]{1,0:T(8,128)(2,1)S(1)} %all_gather.14, bf16[512,2304]{1,0:T(8,128)(2,1)S(1)} %copy-done), kind=kOutput, calls=%fused_computation.28 | convolution fusion | flops 1811939328 | bytes 10223616 | tf_op jit(solution)/shard_map/dot_general | solution.py:19
  200.4 0.0 all-gather.6.cloned.1.call-done
  200.4 20.3 %broadcast_select_fusion = (bf16[768,2304]{1,0:T(8,128)(2,1)}, bf16[768,2304]{1,0:T(8,128)(2,1)}, bf16[768,2304]{1,0:T(8,128)(2,1)}) fusion(bf16[768,2304]{1,0:T(8,128)(2,1)} %param.15, pred[768]{0:T(1024)(128)(4,1)S(1)} %broadcast_compare_fusion, bf16[768,2304]{1,0:T(8,128)(2,1)} %param.12, bf16[768,2304]{1,0:T(8,128)(2,1)} %param.14, ...), kind=kOutput, calls=%fused_computation.7 | convolution fusion | flops 1858338816 | bytes 30673664 | tf_op jit(solution)/shard_map/dot_general | solution.py:55
  (9 shorter events, 0.1 us)
Async XLA Ops:
  7.2 60.0 %all-gather.4.cloned.1.call-start = ((), (), s32[]{:S(2)}) async-start(), calls=%async_computation.2 | async-start | bytes 2506752 | tf_op jit(solution)/shard_map/all_gather | solution.py:36
  26.0 47.8 %copy-start.1 = (s32[768]{0:T(1024)S(1)}, s32[768]{0:T(1024)}, u32[]{:S(2)}) copy-start(s32[768]{0:T(1024)} %param.13) | copy-start | bytes 9220
  26.0 47.8 %copy-start.2 = (s32[16]{0:T(128)S(1)}, s32[16]{0:T(128)}, u32[]{:S(2)}) copy-start(s32[16]{0:T(128)} %param.10) | copy-start | bytes 196
  26.0 47.8 %copy-start.3 = (s32[16]{0:T(128)S(1)}, s32[16]{0:T(128)}, u32[]{:S(2)}) copy-start(s32[16]{0:T(128)} %param.9) | copy-start | bytes 196
  26.1 113.0 %reduce-scatter.2.cloned.1.call-start = ((), (), s32[]{:S(2)}) async-start(), calls=%async_computation.3 | async-start | bytes 2359296 | tf_op jit(solution)/shard_map/reduce_scatter | solution.py:42
  73.0 122.4 %copy-start = (bf16[512,2304]{1,0:T(8,128)(2,1)S(1)}, bf16[512,2304]{1,0:T(8,128)(2,1)}, u32[]{:S(2)}) copy-start(bf16[512,2304]{1,0:T(8,128)(2,1)} %all-gather.4.cloned.1.call-done) | copy-start | bytes 7077892
  73.1 127.3 %all-gather.6.cloned.1.call-start = ((), (), s32[]{:S(2)}) async-start(), calls=%async_computation.4 | async-start | bytes 2506752 | tf_op jit(solution)/shard_map/all_gather | solution.py:37
Sparse Core Ops, SparseCore 0:
  26.1 40.9 all-gather.3
  73.2 26.5 reduce-scatter.1
  102.9 40.8 all-gather.5
where the time goes:
time: 228 us; the launch traced here: 227 us
  blocking collectives  126 us (55%)
  waiting for transfers between devices  41.1 us (18%)
  matrix products  31.1 us (14%)
  between operations  13.9 us (6%)
  local copies, waits for them, and re-layouts  10.4 us (5%)
  other arithmetic  4.81 us (2%)
    all_gather x1, blocking collectives, body(): ids_all = lax.all_gather(both, ('pipe', 'vocab', 'dp'), axis=1, tiled=True)  65 us
    psum x1, blocking collectives, body(): sums = lax.psum(placed, ('pipe', 'dp', 'vocab'))  42 us
    all_gather x1, waiting for transfers between devices, body(): lax.all_gather(packed[0], ('pipe', 'vocab'), axis=0, tiled=True)  41 us
    dot_general x1, matrix products, body(): jnp.dot(selector, grads_all, preferred_element_type=jnp.float32)  20.3 us
    all_gather x1, blocking collectives, body(): dlogits = lax.all_gather(dlogits, 'dp', axis=0, tiled=True)  10.6 us
    all_to_all x1, blocking collectives, body(): lax.all_to_all(jnp.stack([hidden, input_grads]), 'dp', split_axis=2, conc...  8.17 us
    dot_general x1, matrix products, contract_last(): lax.dot_general(left, right, (((1,), (1,)), ((), ())), preferred_element_...  5.88 us
    dot_general x1, matrix products, contract_first(): lax.dot_general(left, right, (((0,), (0,)), ((), ())), preferred_element_...  4.95 us
  transfers between devices with their start and end apart: 3, of which 1 were waited for; matrix products, arithmetic and copies ran while one was open for 4% of the time, Pallas kernels for 0%

commit v1 on v0

--- a/solution.py
+++ b/solution.py
@@ -50,7 +50,15 @@
     total = lax.dynamic_slice(sums[0], (start,), (share,))
     slope = 1.0 - (capped / SOFTCAP) ** 2
     dlogits = ((weights / total[:, None] - onehot) * slope).astype(jnp.bfloat16)
-    dlogits = lax.all_gather(dlogits, "dp", axis=0, tiled=True)
+    ways, here = (lax.axis_size("dp"), lax.axis_index("dp"))
+    grown, reach = (dlogits, 1)
+    while reach < ways:
+        theirs = lax.ppermute(grown, "dp", [(d, d ^ reach) for d in range(ways)])
+        mine_first = jnp.concatenate([grown, theirs], axis=0)
+        theirs_first = jnp.concatenate([theirs, grown], axis=0)
+        grown = jnp.where(here & reach == 0, mine_first, theirs_first)
+        reach = 2 * reach
+    dlogits = grown
     selector = ((ids_all[1] - row_start)[None, :] == row_iota[:, None]).astype(jnp.bfloat16)
     finished = contract_first(dlogits, tokens_all) + scale * jnp.dot(
         selector, grads_all, preferred_element_type=jnp.float32

time: 228 us -> 216 us (0.947)
  blocking collectives: 126 us -> 115 us
  matrix products: 31.1 us -> 26.9 us
    dot_general x1, matrix products: 20.3 us -> 6.75 us  [body(): jnp.dot(selector, grads_all, preferred_element_type=jnp.float32)]
    all_gather x1 -> x0, blocking collectives: 10.6 us -> none  [body(): dlogits = lax.all_gather(dlogits, 'dp', axis=0, tiled=True)]
    dot_general x1, matrix products: 4.95 us -> 14.2 us  [contract_first(): lax.dot_general(left, right, (((0,), (0,)), ((), ())), preferred_element_...]
  transfers between devices with their start and end apart: 3 -> 4, of which waited for: 1 -> 2; matrix products, arithmetic and copies ran while one was open for 4% -> 5% of each run, Pallas kernels for 0% -> 0%
where the time goes in v1:
time: 216 us
  blocking collectives  115 us (53%)
  waiting for transfers between devices  42.9 us (20%)
  matrix products  26.9 us (12%)
  between operations  13.9 us (6%)
  local copies, waits for them, and re-layouts  10.4 us (5%)
  other arithmetic  4.81 us (2%)
    all_gather x1, blocking collectives, body(): ids_all = lax.all_gather(both, ('pipe', 'vocab', 'dp'), axis=1, tiled=True)  65 us
    psum x1, blocking collectives, body(): sums = lax.psum(placed, ('pipe', 'dp', 'vocab'))  42 us
    all_gather x1, waiting for transfers between devices, body(): lax.all_gather(packed[0], ('pipe', 'vocab'), axis=0, tiled=True)  41 us
    dot_general x1, matrix products, contract_first(): lax.dot_general(left, right, (((0,), (0,)), ((), ())), preferred_element_...  14.2 us
    all_to_all x1, blocking collectives, body(): lax.all_to_all(jnp.stack([hidden, input_grads]), 'dp', split_axis=2, conc...  8.17 us
    dot_general x1, matrix products, body(): jnp.dot(selector, grads_all, preferred_element_type=jnp.float32)  6.75 us
    dot_general x1, matrix products, contract_last(): lax.dot_general(left, right, (((1,), (1,)), ((), ())), preferred_element_...  5.88 us
  transfers between devices with their start and end apart: 4, of which 2 were waited for; matrix products, arithmetic and copies ran while one was open for 5% of the time, Pallas kernels for 0%

profile of v1, /device:TPU:10, one launch (start us, length us, event | category | flops | bytes accessed | tf_op | source)
XLA Modules:
  0.0 215.6 jit_solution(8544763584379586176)
XLA Ops:
  7.2 0.0 all-gather.4.cloned.1.call-start
  7.2 1.0 pad_maximum_fusion
  8.2 3.0 %copy.27 = bf16[2,16,4608]{1,0,2:T(2,128)(2,1)S(1)} copy(bf16[2,16,4608]{2,1,0:T(8,128)(2,1)S(1)} %pad_maximum_fusion) | data formatting | bytes 589824 | tf_op jit(solution)/shard_map/stack | solution.py:33
  11.2 2.4 %reshape.30 = bf16[2,2,36864]{2,1,0:T(2,128)(2,1)S(1)} reshape(bf16[4608,2,16]{2,1,0:T(2,128)(2,1)S(1)} %bitcast.26) | data formatting | bytes 589824
  13.7 8.2 %all_to_all.15 = bf16[2,2,36864]{2,1,0:T(2,128)(2,1)S(1)} all-to-all(bf16[2,2,36864]{2,1,0:T(2,128)(2,1)S(1)} %reshape.30), channel_id=1, replica_groups=mesh['pipe'=4,'dp'=2,'vocab'=4] {'dp'}, dimensions={0} | all-to-all | bytes 589824 | tf_op jit(solution)/shard_map/all_to_all | solution.py:32
  21.9 1.6 reshape.31
  23.5 1.6 copy.32
  25.1 0.2 fusion.14
  25.3 0.7 copy.29
  26.0 0.0 all-gather.4.cloned.1.call-update
  26.0 0.0 copy-start
  26.0 0.0 copy-start.1
  26.0 0.0 copy-start.2
  26.1 0.0 reduce-scatter.2.cloned.1.call-start
  26.1 41.0 %all-gather.4.cloned.1.call-done = bf16[512,2304]{1,0:T(8,128)(2,1)} async-done(((bf16[32,2304]{1,0:T(8,128)(2,1)}), bf16[512,2304]{1,0:T(8,128)(2,1)}) %all-gather.4.cloned.1.call-update) | async-done | bytes 2359312 | tf_op jit(solution)/shard_map/all_gather | solution.py:36
  67.1 5.9 %fusion.16 = f32[512,768]{1,0:T(8,128)} fusion(bf16[512,2304]{1,0:T(8,128)(2,1)} %all-gather.4.cloned.1.call-done, bf16[768,2304]{1,0:T(8,128)(2,1)} %param.12), kind=kOutput, calls=%fused_computation.37 | convolution fusion | flops 1811939328 | bytes 7471104 | tf_op jit(solution)/shard_map/dot_general | solution.py:13
  73.0 0.0 reduce-scatter.2.cloned.1.call-update
  73.0 0.0 all-gather.6.cloned.1.call-start
  73.1 0.7 copy.31
  73.8 0.0 all-gather.6.cloned.1.call-update
  73.8 0.0 copy-done
  73.8 0.0 copy-done.1
  73.8 0.0 copy-done.2
  73.9 65.0 %all-gather = s32[32,16,2]{1,2,0:T(2,128)S(1)} all-gather(s32[1,16,2]{1,2,0:T(2,128)S(1)} %add_bitcast_fusion), channel_id=1, replica_groups=mesh['pipe'=4,'dp'=2,'vocab'=4] {'pipe','vocab','dp'}, dimensions={0}, use_global_device_ids=true | all-gather | bytes 4224 | tf_op jit(solution)/shard_map/all_gather | solution.py:35
  138.8 0.1 reshape.29
  139.0 0.0 reduce-scatter.2.cloned.1.call-done
  139.0 1.6 fusion.11
  140.6 42.0 %psum.7 = f32[2,512]{1,0:T(2,128)S(1)} all-reduce(f32[2,512]{1,0:T(2,128)S(1)} %maximum_dynamic-update-slice_fusion), channel_id=1, replica_groups=mesh['pipe'=4,'dp'=2,'vocab'=4] {'pipe','dp','vocab'}, use_global_device_ids=true, to_apply=%region_3.0 | all-reduce | flops 1024 | bytes 8192 | tf_op jit(solution)/shard_map/psum | solution.py:48
  182.6 0.6 fusion.12
  183.2 1.5 multiply_convert_fusion
  184.8 1.4 collective-permute-start
  186.2 0.0 all-gather.6.cloned.1.call-done
  186.2 0.0 copy-start.3
  186.2 0.0 copy-start.4
  186.2 0.0 copy-start.5
  186.2 6.8 %fusion.3 = f32[768,2304]{1,0:T(8,128)} fusion(bf16[512,2304]{1,0:T(8,128)(2,1)} %all-gather.6.cloned.1.call-done, s32[512]{0:T(512)S(1)} %bitcast.39), kind=kOutput, calls=%fused_computation.10 | convolution fusion | flops 1812332544 | bytes 9439232 | tf_op jit(solution)/shard_map/dot_general | solution.py:63
  193.0 1.8 collective-permute-done
  194.8 0.0 copy-done.3
  194.8 0.0 copy-done.4
  194.8 0.0 copy-done.5
  194.8 14.2 %broadcast_select_fusion = (bf16[768,2304]{1,0:T(8,128)(2,1)}, bf16[768,2304]{1,0:T(8,128)(2,1)}, bf16[768,2304]{1,0:T(8,128)(2,1)}) fusion(bf16[768,2304]{1,0:T(8,128)(2,1)S(1)} %copy-done.3, pred[768]{0:T(1024)(128)(4,1)S(1)} %broadcast_compare_fusion, bf16[768,2304]{1,0:T(8,128)(2,1)S(1)} %copy-done.4, bf16[768,2304]{1,0:T(8,128)(2,1)} %param.14, ...), kind=kOutput, calls=%fused_computation.7 | convolution fusion | flops 1861484544 | bytes 31458048 | tf_op jit(solution)/shard_map/dot_general | solution.py:19
  (9 shorter events, 0.1 us)
Async XLA Ops:
  7.2 60.0 %all-gather.4.cloned.1.call-start = ((), (), s32[]{:S(2)}) async-start(), calls=%async_computation.2 | async-start | bytes 2506752 | tf_op jit(solution)/shard_map/all_gather | solution.py:36
  26.0 47.8 %copy-start = (s32[768]{0:T(1024)S(1)}, s32[768]{0:T(1024)}, u32[]{:S(2)}) copy-start(s32[768]{0:T(1024)} %param.13) | copy-start | bytes 9220
  26.0 47.8 %copy-start.1 = (s32[16]{0:T(128)S(1)}, s32[16]{0:T(128)}, u32[]{:S(2)}) copy-start(s32[16]{0:T(128)} %param.10) | copy-start | bytes 196
  26.0 47.8 %copy-start.2 = (s32[16]{0:T(128)S(1)}, s32[16]{0:T(128)}, u32[]{:S(2)}) copy-start(s32[16]{0:T(128)} %param.9) | copy-start | bytes 196
  26.1 113.0 %reduce-scatter.2.cloned.1.call-start = ((), (), s32[]{:S(2)}) async-start(), calls=%async_computation.3 | async-start | bytes 2359296 | tf_op jit(solution)/shard_map/reduce_scatter | solution.py:42
  73.0 113.2 %all-gather.6.cloned.1.call-start = ((), (), s32[]{:S(2)}) async-start(), calls=%async_computation.4 | async-start | bytes 2506752 | tf_op jit(solution)/shard_map/all_gather | solution.py:37
  184.8 10.0 %collective-permute-start = (bf16[256,768]{1,0:T(8,128)(2,1)S(1)}, bf16[256,768]{1,0:T(8,128)(2,1)S(1)}, u32[]{:S(2)}, u32[]{:S(2)}) collective-permute-start(bf16[256,768]{1,0:T(8,128)(2,1)S(1)} %multiply_convert_fusion), channel_id=1, source_target_pairs={{0,4},{4,0},{1,5},{5,1},{2,6},{6,2},{3,7},{7,3},{8,12},{12,8},{9,1... | collective-permute-start | bytes 1179656 | tf_op jit(solution)/shard_map/ppermute | solution.py:56
  186.2 8.6 %copy-start.3 = (bf16[768,2304]{1,0:T(8,128)(2,1)S(1)}, bf16[768,2304]{1,0:T(8,128)(2,1)}, u32[]{:S(2)}) copy-start(bf16[768,2304]{1,0:T(8,128)(2,1)} %param.15) | copy-start | bytes 10616836
  186.2 8.6 %copy-start.4 = (bf16[768,2304]{1,0:T(8,128)(2,1)S(1)}, bf16[768,2304]{1,0:T(8,128)(2,1)}, u32[]{:S(2)}) copy-start(bf16[768,2304]{1,0:T(8,128)(2,1)} %param.12) | copy-start | bytes 10616836
  186.2 8.6 %copy-start.5 = (bf16[512,2304]{1,0:T(8,128)(2,1)S(1)}, bf16[512,2304]{1,0:T(8,128)(2,1)}, u32[]{:S(2)}) copy-start(bf16[512,2304]{1,0:T(8,128)(2,1)} %all-gather.4.cloned.1.call-done) | copy-start | bytes 7077892
Sparse Core Ops, SparseCore 0:
  26.1 40.9 all-gather.3
  73.2 26.5 reduce-scatter.1
  102.9 40.8 all-gather.5
